TPU v7x, 32 devices: a whole 2x2x4 slice. The times are simulated.
32 devices in a mesh: groups: 2 (over x), docs: 16 (over z, y, core).
Axes of the slice: x: 2, y: 2, z: 4, core: 2. Of those that a mesh axis runs over, the one named last changes fastest.
Arguments:
- query_act: bfloat16 [8, 16, 8192], P('groups'), parts along dimension 0, may hold values from -6 to 6
- query_grad: bfloat16 [8, 16, 7168], P('groups', None, 'docs'), parts along dimension 0, may hold values from -6 to 6
- eigenvalues: bfloat16 [8192, 7168], P(None, 'docs'), may hold values from 0.049804688 to 1
- doc_act: bfloat16 [32, 6, 8192], P(('groups', 'docs')), parts along dimension 0, may hold values from -6 to 6
- doc_grad: bfloat16 [32, 6, 7168], P(('groups', 'docs')), parts along dimension 0, may hold values from -6 to 6
- doc_len: int32 [32], P(('groups', 'docs')), parts along dimension 0, may hold values from 1 to 6, 56 in all
Outputs:
- scores: float32 [4, 32], P(None, ('groups', 'docs')), parts along dimension 1
There are 2 independent parts, one for each index of `groups`. A program takes and returns all parts, laid end to end along the dimension named above; an argument that names none is the same for every part. Nothing has to cross between parts.
Inputs may be any that keep to these rules, and one draw needn't show every extreme that they name: `doc_len`: token counts of the documents; at least one document has all 6 slots live.
All inputs are finite; a program needn't handle non-finite values. No bound on the sum of `doc_len` on one device may be relied on, other than what follows from the above.
Results may differ from a plain program's by a relative error of at most 0.0035.
Values may be sent and summed in bfloat16 or wider, within the bound.
A program may use at most 192 MiB of HBM per device.

v0:
```python
import math

import jax
import jax.numpy as jnp
from jax import lax
from jax.sharding import PartitionSpec as P

damping = 0.05


def body(query_act, query_grad, eigenvalues, doc_act, doc_grad, doc_len):
    queries = query_act.shape[0]
    qtokens = query_act.shape[1]
    model_width = doc_act.shape[2]
    doc_slots = doc_act.shape[1]
    slab_width = eigenvalues.shape[1]
    devices = lax.axis_size("docs")
    all_units = slab_width * devices
    own_docs = doc_act.shape[0]
    positions = jnp.arange(doc_slots, dtype=jnp.int32)
    alive_mask = positions[None, :] < doc_len[:, None]
    masked = jnp.where(alive_mask[:, :, None], doc_grad, jnp.zeros((), doc_grad.dtype))
    grad_slab = lax.all_to_all(masked, "docs", split_axis=2, concat_axis=0, tiled=True)
    gathered = lax.all_gather(doc_act, "docs", axis=0, tiled=True)
    damped = eigenvalues.astype(jnp.float32) + damping
    blocks = []
    for query in range(queries):
        gram = lax.dot_general(
            query_act[query],
            query_grad[query],
            (((0,), (0,)), ((), ())),
            preferred_element_type=jnp.float32,
        )
        blocks.append((gram / damped).astype(jnp.bfloat16))
    precond = jnp.concatenate(blocks, axis=1)
    doc_count = gathered.shape[0]
    image = jnp.dot(
        gathered.reshape(doc_count * doc_slots, model_width),
        precond,
        preferred_element_type=jnp.float32,
    )
    image = image.reshape(doc_count, doc_slots, queries, slab_width)
    weighted = jnp.sum(image * grad_slab[:, :, None, :], axis=(1, 3))
    partial_scores = weighted.T
    norm_factor = 1.0 / (5.0 * math.sqrt(qtokens * model_width * all_units * doc_slots))
    summed = lax.psum(partial_scores, "docs")
    own_scores = lax.dynamic_slice_in_dim(summed, lax.axis_index("docs") * own_docs, own_docs, 1)
    return own_scores * norm_factor


def solution(mesh):
    in_specs = (
        P("groups", None, None),
        P("groups", None, "docs"),
        P(None, "docs"),
        P(("groups", "docs"), None, None),
        P(("groups", "docs"), None, None),
        P(("groups", "docs")),
    )
    out_specs = P(None, ("groups", "docs"))
    return jax.shard_map(body, mesh=mesh, in_specs=in_specs, out_specs=out_specs, check_vma=False)
```

profile of v0, /device:TPU:0, one launch (start us, length us, event | category | flops | bytes accessed | tf_op | source)
XLA Modules:
  0.0 161.9 jit_solution(5045578963356518750)
XLA Ops:
  6.5 0.7 all-gather.2.cloned.1.call-update
  7.9 1.0 broadcast_select_fusion
  8.9 6.1 %copy.13 = bf16[1,6,7168]{1,0,2:T(2,128)(2,1)} copy(bf16[1,6,7168]{2,1,0:T(8,128)(2,1)S(1)} %broadcast_select_fusion) | data formatting | bytes 172032 | tf_op jit(solution)/shard_map/jit(_where)/select_n | solution.py:22
  15.0 0.5 broadcast.13
  15.5 39.8 %reduce = bf16[7168,6]{1,0:T(8,128)(2,1)S(1)} reduce(bf16[7168,1,6]{2,1,0:T(2,128)(2,1)} %bitcast.39, bf16[]{:T(256)} %broadcast.13), dimensions={1}, to_apply=%bitcast.33.reduce_sub_computation | reduce | bytes 172034
  55.3 4.0 %reshape.33 = bf16[16,2,1344]{2,1,0:T(2,128)(2,1)} reshape(bf16[7168,6]{1,0:T(8,128)(2,1)S(1)} %reduce) | data formatting | bytes 172032
  59.3 7.4 %all-to-all-start = ((bf16[16,2,1344]{2,1,0:T(2,128)(2,1)}), bf16[16,2,1344]{2,1,0:T(2,128)(2,1)S(1)}, u32[]{:S(2)}, u32[]{:S(2)}) async-start(bf16[16,2,1344]{2,1,0:T(2,128)(2,1)} %reshape.33), calls=%async_computation | async-start | bytes 180224 | tf_op jit(solution)/shard_map/all_to_all | solution.py:23
  66.8 0.0 slice-start
  66.8 6.5 %divide_convert_fusion = bf16[8192,448]{0,1:T(8,128)(2,1)} fusion(bf16[8192,448]{0,1:T(8,128)(2,1)} %param.8, bf16[4,16,8192]{2,1,0:T(8,128)(2,1)S(1)} %copy-done, bf16[4,16,448]{2,1,0:T(8,128)(2,1)S(1)} %copy-done.1), kind=kOutput, calls=%fused_computation.8 | convolution fusion | flops 132120576 | bytes 14958592 | tf_op jit(solution)/shard_map/dot_general | solution.py:28
  73.3 6.5 %divide_convert_fusion.1 = bf16[8192,448]{0,1:T(8,128)(2,1)} fusion(bf16[8192,448]{0,1:T(8,128)(2,1)} %param.8, bf16[4,16,8192]{2,1,0:T(8,128)(2,1)S(1)} %copy-done, bf16[4,16,448]{2,1,0:T(8,128)(2,1)S(1)} %copy-done.1), kind=kOutput, calls=%fused_computation.9 | convolution fusion | flops 132120576 | bytes 14958592 | tf_op jit(solution)/shard_map/dot_general | solution.py:28
  79.8 0.0 slice-done.1
  79.9 4.4 %divide_convert_fusion.2 = bf16[8192,448]{0,1:T(8,128)(2,1)} fusion(bf16[8192,448]{0,1:T(8,128)(2,1)S(1)} %bitcast.42, bf16[4,16,8192]{2,1,0:T(8,128)(2,1)S(1)} %copy-done, bf16[4,16,448]{2,1,0:T(8,128)(2,1)S(1)} %copy-done.1), kind=kOutput, calls=%fused_computation.10 | convolution fusion | flops 132120576 | bytes 14958592 | tf_op jit(solution)/shard_map/dot_general | solution.py:28
  84.2 4.4 %divide_convert_fusion.3 = bf16[8192,448]{0,1:T(8,128)(2,1)} fusion(bf16[8192,448]{0,1:T(8,128)(2,1)S(1)} %bitcast.42, bf16[4,16,8192]{2,1,0:T(8,128)(2,1)S(1)} %copy-done, bf16[4,16,448]{2,1,0:T(8,128)(2,1)S(1)} %copy-done.1), kind=kOutput, calls=%fused_computation.11 | convolution fusion | flops 132120576 | bytes 14958592 | tf_op jit(solution)/shard_map/dot_general | solution.py:28
  88.6 0.0 all-to-all-done
  88.6 5.8 %reshape.34 = bf16[7168,1,6]{2,1,0:T(2,128)(2,1)} reshape(bf16[16,2,1344]{2,1,0:T(2,128)(2,1)S(1)} %all-to-all-done) | data formatting | bytes 172032
  94.4 7.7 %bitcast_convert_fusion = f32[1,6,7168]{1,0,2:T(1,128)} fusion(bf16[7168,1,6]{2,1,0:T(2,128)(2,1)} %reshape.34), kind=kLoop, calls=%fused_computation.35 | loop fusion | flops 43008 | bytes 258048 | tf_op jit(solution)/shard_map/convert_element_type | solution.py:43
  102.1 2.7 %copy.14 = f32[16,6,448]{2,1,0:T(8,128)S(1)} copy(f32[16,6,448]{1,2,0:T(8,128)} %bitcast.38) | data formatting | bytes 344064 | tf_op jit(solution)/shard_map/convert_element_type | solution.py:43
  104.9 0.0 all-gather.2.cloned.1.call-done
  104.9 1.9 %reshape.29 = bf16[96,8192]{1,0:T(8,128)(2,1)S(1)} reshape(bf16[16,6,8192]{2,1,0:T(8,128)(2,1)} %all-gather.2.cloned.1.call-done) | data formatting | bytes 3145728 | tf_op jit(solution)/shard_map/reshape | solution.py:38
  106.8 12.4 %fusion.8 = f32[96,1792]{1,0:T(8,128)S(1)} fusion(bf16[96,8192]{1,0:T(8,128)(2,1)S(1)} %reshape.29, bf16[8192,448]{0,1:T(8,128)(2,1)} %divide_convert_fusion, bf16[8192,448]{0,1:T(8,128)(2,1)} %divide_convert_fusion.1, bf16[8192,448]{0,1:T(8,128)(2,1)} %divide_convert_fusion.2, bf16[8192,448]{0,1:T(8,128)(2,1)} %divide_convert_fusion.3), kind=kOutput, calls=%fused_computation.13 | convolution fusion | flops 2936012800 | bytes 31621120 | tf_op jit(solution)/shard_map/dot_general | solution.py:37
  119.1 0.7 reshape.30
  119.9 0.3 multiply_reduce_fusion
  120.2 34.3 %psum.7 = f32[4,16]{0,1:T(8,128)S(1)} all-reduce(f32[4,16]{0,1:T(8,128)S(1)} %bitcast.40), channel_id=1, replica_groups=mesh['groups'=2,'docs'=16] {'docs'}, use_global_device_ids=true, to_apply=%region_1.2 | all-reduce | flops 64 | bytes 512 | tf_op jit(solution)/shard_map/psum | solution.py:46
  154.5 0.5 dynamic-slice_multiply_fusion
  (9 shorter events, 0.0 us)
Async XLA Ops:
  6.5 60.2 %copy-start = (bf16[4,16,8192]{2,1,0:T(8,128)(2,1)S(1)}, bf16[4,16,8192]{2,1,0:T(8,128)(2,1)}, u32[]{:S(2)}) copy-start(bf16[4,16,8192]{2,1,0:T(8,128)(2,1)} %param.6) | copy-start | bytes 3145732
  6.5 60.2 %copy-start.1 = (bf16[4,16,448]{2,1,0:T(8,128)(2,1)S(1)}, bf16[4,16,448]{2,1,0:T(8,128)(2,1)}, u32[]{:S(2)}) copy-start(bf16[4,16,448]{2,1,0:T(8,128)(2,1)} %param.7) | copy-start | bytes 172036
  6.5 98.3 %all-gather.2.cloned.1.call-start = ((), (), s32[]{:S(2)}) async-start(), calls=%async_computation.1 | async-start | bytes 2228224 | tf_op jit(solution)/shard_map/all_gather | solution.py:24
  59.3 29.3 %all-to-all-start = ((bf16[16,2,1344]{2,1,0:T(2,128)(2,1)}), bf16[16,2,1344]{2,1,0:T(2,128)(2,1)S(1)}, u32[]{:S(2)}, u32[]{:S(2)}) async-start(bf16[16,2,1344]{2,1,0:T(2,128)(2,1)} %reshape.33), calls=%async_computation | async-start | bytes 180224 | tf_op jit(solution)/shard_map/all_to_all | solution.py:23
  66.8 13.1 %slice-start = ((s8[7340032]{0:T(1024)(128)(4,1)}), s8[4194304]{0:T(1024)(128)(4,1)S(1)}, s32[]{:S(2)}) async-start(s8[7340032]{0:T(1024)(128)(4,1)} %bitcast.41), calls=%async_computation.2 | async-start | bytes 8388608
  73.3 6.5 %slice-start.1 = ((s8[7340032]{0:T(1024)(128)(4,1)}), s8[3145728]{0:T(1024)(128)(4,1)S(1)}, s32[]{:S(2)}) async-start(s8[7340032]{0:T(1024)(128)(4,1)} %bitcast.41), calls=%async_computation.3 | async-start | bytes 6291456
Sparse Core Ops, SparseCore 0:
  9.5 44.0 all-gather.1
where the time goes:
time: 162 us
  other arithmetic  49.3 us (30%)
  blocking collectives  34.3 us (21%)
  matrix products  34.2 us (21%)
  local copies, waits for them, and re-layouts  21.8 us (13%)
  between operations  14.1 us (9%)
  starting transfers between devices  7.4 us (5%)
    unnamed x2, other arithmetic  39.8 us
    psum x1, blocking collectives, body(): summed = lax.psum(partial_scores, 'docs')  34.3 us
    dot_general x4, matrix products, body(): lax.dot_general(query_act[query], query_grad[query], (((0,), (0,)), ((),...  21.8 us
    dot_general x1, matrix products, body(): jnp.dot(gathered.reshape(doc_count * doc_slots, model_width), precond, pr...  12.4 us
    unnamed x11, local copies, waits for them, and re-layouts  10.3 us
    convert_element_type x1, other arithmetic, body(): weighted = jnp.sum(image * grad_slab[:, :, None, :], axis=(1, 3))  7.75 us
    all_to_all x1, starting transfers between devices, body(): lax.all_to_all(masked, 'docs', split_axis=2, concat_axis=0, tiled=True)  7.39 us
    select_n x1, local copies, waits for them, and re-layouts, body(): jnp.where(alive_mask[:, :, None], doc_grad, jnp.zeros((), doc_grad.dtype))  6.1 us
  transfers between devices with their start and end apart: 2, of which 0 were waited for; matrix products, arithmetic and copies ran while one was open for 55% of the time, Pallas kernels for 0%

commit v1 on v0

v1 whole, which is shorter than its diff:
```python
import functools
import math

import jax
import jax.numpy as jnp
from jax import lax
from jax.experimental import pallas as pl
from jax.experimental.pallas import tpu as pltpu
from jax.sharding import PartitionSpec as P

damping = 0.05
MESH = pl.DeviceIdType.MESH
f32 = jnp.float32
bf16 = jnp.bfloat16

FOLDS = 8
CHUNK = 256
EIG_SLOTS = 4


def kernel(n, scale, len_ref, qact_ref, qgrad_ref, eig_ref, dact_ref, dgrad_ref, out_ref,
           buf, wide, actb, pre, eigv, qt, bd, own, gown, gtmp, gsend, grecv, gwide, acc, part, parts,
           eig_sem, ring_send, ring_recv, cross_send, cross_recv, g_send, g_recv, p_send, p_recv):
    queries, qtokens, width = qact_ref.shape
    tokens = dact_ref.shape[1]
    slab = eig_ref.shape[1]
    fold = width // FOLDS
    half = fold // 2
    full = slab // 128
    chips = n // 2
    hops = chips // 2
    groups = chips
    group_rows = width // groups
    me = lax.axis_index("docs")
    core = lax.rem(me, 2)
    chip = me // 2
    snake = n == 16

    if snake:
        pos = chip // 2 + lax.rem(chip, 2) * (chips - 1 - 2 * (chip // 2))
    else:
        pos = chip

    def device_at(p, c):
        p = lax.rem(p + 2 * chips, chips)
        if snake:
            y = p // hops
            return 2 * (2 * (p + y * (chips - 1 - 2 * p)) + y) + c
        return 2 * p + c

    def eig_copy(g):
        slot = lax.rem(g, EIG_SLOTS)
        return pltpu.make_async_copy(
            eig_ref.at[pl.ds(pl.multiple_of(g * group_rows, group_rows), group_rows)],
            eigv.at[slot], eig_sem.at[slot])

    for g in range(EIG_SLOTS - 1):
        eig_copy(g).start()

    barrier = pltpu.get_barrier_semaphore()

    @pl.loop(1, n)
    def _(r):
        pl.semaphore_signal(barrier, inc=1, device_id={"docs": lax.rem(me + r, n)}, device_id_type=MESH)

    mine = dact_ref[0].astype(f32)
    for k in range(FOLDS):
        for b in range(fold // 128):
            at = k * fold + b * 128
            own[b, pl.ds(k, tokens, stride=FOLDS), :] = mine[:, at:at + 128]
    for b in range(fold // 128):
        buf[me, :, b * 128:(b + 1) * 128] = own[b].astype(bf16)

    def ring_copy(way, step, h):
        sign = 1 - 2 * way
        block = device_at(pos - sign * (step - 1), core)
        view = buf.at[block, :, pl.ds(pl.multiple_of(h * half, half), half)]
        return pltpu.make_async_remote_copy(
            src_ref=view, dst_ref=view,
            send_sem=ring_send.at[way, step - 1, h], recv_sem=ring_recv.at[way, step - 1, h],
            device_id={"docs": device_at(pos + sign, core)}, device_id_type=MESH)

    def ring_arrival(way, step, h):
        sign = 1 - 2 * way
        block = device_at(pos - sign * step, core)
        view = buf.at[block, :, pl.ds(pl.multiple_of(h * half, half), half)]
        return pltpu.make_async_remote_copy(
            src_ref=view, dst_ref=view,
            send_sem=ring_send.at[way, step - 1, h], recv_sem=ring_recv.at[way, step - 1, h],
            device_id={"docs": device_at(pos + sign, core)}, device_id_type=MESH)

    def cross_copy(p, c):
        p = lax.rem(p + 2 * chips, chips)
        view = buf.at[device_at(p, c)]
        return pltpu.make_async_remote_copy(
            src_ref=view, dst_ref=view,
            send_sem=cross_send.at[p], recv_sem=cross_recv.at[p],
            device_id={"docs": 2 * chip + 1 - core}, device_id_type=MESH)

    pl.semaphore_wait(barrier, n - 1)
    for h in range(2):
        for way in range(2):
            ring_copy(way, 1, h).start()
    cross_copy(pos, core).start()

    bd[...] = jnp.zeros_like(bd)
    for q in range(queries):
        rows = slice(q * qtokens, (q + 1) * qtokens)
        for j in range(full):
            at = (j * queries + q) * 128
            bd[rows, at:at + 128] = qgrad_ref[q, :, j * 128:(j + 1) * 128]
        rest = qgrad_ref[q, :, full * 128:]
        none = jnp.zeros_like(rest)
        at = (full * queries + q // 2) * 128
        bd[rows, at:at + 128] = jnp.concatenate([rest, none] if q % 2 == 0 else [none, rest], axis=1)
    for q in range(queries):
        rows = slice(q * qtokens, (q + 1) * qtokens)
        qt[rows, :] = qact_ref[q]

    def make_pre(g):
        slot = lax.rem(g, EIG_SLOTS)
        eig_copy(g).wait()

        @pl.when(g + EIG_SLOTS - 1 < groups)
        def _():
            eig_copy(g + EIG_SLOTS - 1).start()

        @pl.loop(0, group_rows // CHUNK)
        def _(c):
            local = pl.multiple_of(c * CHUNK, CHUNK)
            at = pl.multiple_of(g * group_rows + c * CHUNK, CHUNK)
            left = qt[:, pl.ds(at, CHUNK)].T
            inv = 1.0 / (eigv[slot, pl.ds(local, CHUNK), :].astype(f32) + damping)
            tail = inv[:, full * 128:]
            tail = jnp.concatenate([tail, tail], axis=1)
            for pair in range(bd.shape[1] // 256):
                cols = slice(pair * 256, pair * 256 + 256)
                gram = jnp.dot(left, bd[:, cols], preferred_element_type=f32)
                for side in range(2):
                    j = (pair * 2 + side) // queries
                    w = inv[:, j * 128:(j + 1) * 128] if j < full else tail
                    lo = pair * 256 + side * 128
                    pre[pl.ds(at, CHUNK), lo:lo + 128] = (gram[:, side * 128:side * 128 + 128] * w).astype(bf16)

    @pl.loop(0, chips - 2)
    def _(e):
        make_pre(e)
        step = e // 2 + 1
        h = lax.rem(e, 2)
        for way in range(2):
            ring_arrival(way, step, h).wait_recv()

            @pl.when(step + 1 < hops)
            def _():
                ring_copy(way, step + 1, h).start()

        @pl.when(e == chips - 4)
        def _():
            ring_copy(0, hops, 0).start()

        @pl.when(e == chips - 3)
        def _():
            ring_copy(1, hops, 1).start()

        @pl.when(h == 1)
        def _():
            cross_copy(pos - step, core).start()
            cross_copy(pos + step, core).start()

    slot_of = lax.broadcasted_iota(jnp.int32, (tokens, dgrad_ref.shape[2]), 0)
    gown[...] = jnp.where(slot_of < len_ref[0], dgrad_ref[0].astype(f32), 0.0)
    gtmp[...] = jnp.zeros_like(gtmp)

    def g_copy(slot, to):
        return pltpu.make_async_remote_copy(
            src_ref=gsend.at[to], dst_ref=grecv.at[slot],
            send_sem=g_send.at[to], recv_sem=g_recv.at[slot],
            device_id={"docs": to}, device_id_type=MESH)

    @pl.loop(0, n)
    def _(r):
        to = lax.rem(me + r, n)
        start = pl.multiple_of((to * slab) // 128 * 128, 128)
        for side in range(2):
            for b in range(2):
                at = pl.multiple_of(start + side * 256 + b * 128, 128)
                gtmp[b, pl.ds(side, tokens, stride=2), :] = gown[:, pl.ds(at, 128)]
        cut = jnp.concatenate([gtmp[0], gtmp[1]], axis=1).astype(bf16)
        gsend[to] = cut

        @pl.when(r == 0)
        def _():
            grecv[me] = cut

        @pl.when(r > 0)
        def _():
            g_copy(me, to).start()

    make_pre(chips - 2)
    ring_arrival(0, hops, 0).wait_recv()
    ring_arrival(1, hops, 1).wait_recv()
    cross_copy(pos + hops, core).start()
    make_pre(chips - 1)

    @pl.loop(0, chips)
    def _(p):
        cross_copy(p, 1 - core).wait_recv()

    @pl.loop(0, n)
    def _(d):
        block = buf[d].astype(f32)
        for t in range(tokens):
            at = pl.ds(pl.multiple_of((t * n + d) * FOLDS, FOLDS), FOLDS)
            for b in range(fold // 128):
                wide[b, at, :] = block[t * FOLDS:(t + 1) * FOLDS, b * 128:(b + 1) * 128]


    acc[...] = jnp.zeros_like(acc)

    @pl.loop(0, FOLDS)
    def _(k):
        rows = pl.ds(pl.multiple_of(k * fold, fold), fold)
        for b in range(fold // 128):
            actb[:, b * 128:(b + 1) * 128] = wide[b, pl.ds(k, tokens * n, stride=FOLDS), :].astype(bf16)
        for pair in range(bd.shape[1] // 256):
            cols = slice(pair * 256, pair * 256 + 256)
            acc[:, cols] += jnp.dot(actb[...], pre[rows, cols], preferred_element_type=f32)

    @pl.loop(1, n)
    def _(r):
        g_copy(lax.rem(me + r, n), me).wait_recv()

    @pl.loop(0, n)
    def _(d):
        got = grecv[d].astype(f32)
        for b in range(2):
            gwide[b, pl.ds(pl.multiple_of(d * 16, 16), 16), :] = got[:, b * 128:(b + 1) * 128]

    part[...] = jnp.zeros_like(part)
    odd = lax.rem(me, 2) == 1
    sums = [jnp.zeros((n, 128), f32) for _ in range(queries)]
    low = lax.broadcasted_iota(jnp.int32, (n, 128), 1) < slab - full * 128
    for t in range(tokens):
        window = jnp.concatenate(
            [gwide[b, pl.ds(t * 2 + side, n, stride=16), :] for side in range(2) for b in range(2)], axis=1)
        moved = jnp.concatenate([window[:, 64:], window[:, :64]], axis=1)
        grad = jnp.where(odd, moved, window)
        last = grad[:, full * 128:full * 128 + 64]
        last = jnp.concatenate([last, last], axis=1)
        rows = slice(t * n, (t + 1) * n)
        for q in range(queries):
            for j in range(full):
                at = (j * queries + q) * 128
                sums[q] += acc[rows, at:at + 128] * grad[:, j * 128:(j + 1) * 128]
            at = (full * queries + q // 2) * 128
            both = acc[rows, at:at + 128] * last
            sums[q] += jnp.where(low if q % 2 == 0 else jnp.logical_not(low), both, 0.0)
    for q in range(queries):
        part[pl.ds(q, n, stride=8), :] = sums[q]

    def p_copy(slot, to):
        return pltpu.make_async_remote_copy(
            src_ref=part.at[pl.ds(pl.multiple_of(to * 8, 8), 8)],
            dst_ref=parts.at[pl.ds(pl.multiple_of(slot * 8, 8), 8)],
            send_sem=p_send.at[to], recv_sem=p_recv.at[slot],
            device_id={"docs": to}, device_id_type=MESH)

    @pl.loop(1, n)
    def _(r):
        p_copy(me, lax.rem(me + r, n)).start()

    mine_at = pl.ds(pl.multiple_of(me * 8, 8), 8)
    parts[mine_at, :] = part[mine_at, :]

    for h in range(2):
        for way in range(2):
            @pl.loop(1, hops)
            def _(s):
                ring_copy(way, s, h).wait_send()
    ring_copy(0, hops, 0).wait_send()
    ring_copy(1, hops, 1).wait_send()

    @pl.loop(0, chips)
    def _(p):
        cross_copy(p, core).wait_send()

    @pl.loop(1, n)
    def _(r):
        g_copy(me, lax.rem(me + r, n)).wait_send()

    @pl.loop(1, n)
    def _(r):
        p_copy(lax.rem(me + r, n), me).wait_recv()

    total = parts[0:8, :]
    for d in range(1, n):
        total += parts[d * 8:d * 8 + 8, :]
    out_ref[...] = jnp.sum(total, axis=1, keepdims=True)[:queries] * scale

    @pl.loop(1, n)
    def _(r):
        p_copy(me, lax.rem(me + r, n)).wait_send()


def body(query_act, query_grad, eigenvalues, doc_act, doc_grad, doc_len):
    queries, qtokens, width = query_act.shape
    tokens = doc_act.shape[1]
    slab = eigenvalues.shape[1]
    n = lax.axis_size("docs")
    chips = n // 2
    fold = width // FOLDS
    columns = queries * slab
    scale = 1.0 / (5.0 * math.sqrt(qtokens * width * slab * n * tokens))
    vmem = pl.BlockSpec(memory_space=pltpu.VMEM)
    dma = pltpu.SemaphoreType.DMA
    return pl.pallas_call(
        functools.partial(kernel, n, scale),
        out_shape=jax.ShapeDtypeStruct((queries, 1), f32),
        in_specs=[pl.BlockSpec(memory_space=pltpu.SMEM), vmem, vmem, pl.BlockSpec(memory_space=pl.ANY), vmem, vmem],
        out_specs=vmem,
        scratch_shapes=[
            pltpu.VMEM((n, tokens * FOLDS, fold), bf16),
            pltpu.VMEM((fold // 128, n * tokens * FOLDS, 128), f32),
            pltpu.VMEM((n * tokens, fold), bf16),
            pltpu.VMEM((width, columns), bf16),
            pltpu.VMEM((EIG_SLOTS, width // chips, slab), bf16),
            pltpu.VMEM((queries * qtokens, width), bf16),
            pltpu.VMEM((queries * qtokens, columns), bf16),
            pltpu.VMEM((fold // 128, tokens * FOLDS, 128), f32),
            pltpu.VMEM((tokens, doc_grad.shape[2]), f32),
            pltpu.VMEM((2, 16, 128), f32),
            pltpu.VMEM((n, 16, 256), bf16),
            pltpu.VMEM((n, 16, 256), bf16),
            pltpu.VMEM((2, n * 16, 128), f32),
            pltpu.VMEM((n * tokens, columns), f32),
            pltpu.VMEM((n * 8, 128), f32),
            pltpu.VMEM((n * 8, 128), f32),
            dma((EIG_SLOTS,)),
            dma((2, chips // 2, 2)),
            dma((2, chips // 2, 2)),
            dma((chips,)),
            dma((chips,)),
            dma((n,)),
            dma((n,)),
            dma((n,)),
            dma((n,)),
        ],
        compiler_params=pltpu.CompilerParams(
            collective_id=0, has_side_effects=True, vmem_limit_bytes=62 * 1024 * 1024),
    )(doc_len, query_act, query_grad, eigenvalues, doc_act, doc_grad)


def solution(mesh):
    in_specs = (
        P("groups", None, None),
        P("groups", None, "docs"),
        P(None, "docs"),
        P(("groups", "docs"), None, None),
        P(("groups", "docs"), None, None),
        P(("groups", "docs")),
    )
    out_specs = P(None, ("groups", "docs"))
    return jax.shard_map(body, mesh=mesh, in_specs=in_specs, out_specs=out_specs, check_vma=False)
```

time: 162 us -> 51.8 us (0.32)
  other arithmetic: 49.3 us -> 0 us
  Pallas kernels: 0 us -> 37.8 us
  blocking collectives: 34.3 us -> 0 us
  matrix products: 34.2 us -> 0 us
  between operations: 14.1 us -> 0.66 us
  local copies, waits for them, and re-layouts: 21.8 us -> 12.8 us
  starting transfers between devices: 7.4 us -> 0 us
    unnamed x2 -> x0, other arithmetic: 39.8 us -> none
    pallas_call x0 -> x1, Pallas kernels: none -> 37.8 us  [body(): pl.pallas_call(functools.partial(kernel, n, scale), out_shape=jax.ShapeDt...]
    psum x1 -> x0, blocking collectives: 34.3 us -> none  [body(): summed = lax.psum(partial_scores, 'docs')]
    dot_general x5 -> x0, matrix products: 34.2 us -> none  [the longest x4 21.8 us: body(): lax.dot_general(query_act[query], query_grad[query], (((0,), (0,)), ((),...]
    convert_element_type x1 -> x0, other arithmetic: 7.75 us -> none  [body(): weighted = jnp.sum(image * grad_slab[:, :, None, :], axis=(1, 3))]
    all_to_all x1 -> x0, starting transfers between devices: 7.39 us -> none  [body(): lax.all_to_all(masked, 'docs', split_axis=2, concat_axis=0, tiled=True)]
    select_n x1 -> x0, local copies, waits for them, and re-layouts: 6.1 us -> none  [body(): jnp.where(alive_mask[:, :, None], doc_grad, jnp.zeros((), doc_grad.dtype))]
    convert_element_type x1 -> x0, local copies, waits for them, and re-layouts: 2.75 us -> none  [body(): weighted = jnp.sum(image * grad_slab[:, :, None, :], axis=(1, 3))]
  transfers between devices with their start and end apart: 2 -> 0, of which waited for: 0 -> 0; matrix products, arithmetic and copies ran while one was open for 55% -> 0% of each run, Pallas kernels for 0% -> 0%
where the time goes in v1:
time: 51.8 us; the launch traced here: 51.3 us
  Pallas kernels  37.8 us (73%)
  local copies, waits for them, and re-layouts  12.8 us (25%)
  between operations  0.66 us (1%)
    pallas_call x1, Pallas kernels, body(): pl.pallas_call(functools.partial(kernel, n, scale), out_shape=jax.ShapeDt...  37.8 us
    unnamed x1, local copies, waits for them, and re-layouts  11.6 us
    pallas_call x1, local copies, waits for them, and re-layouts, body(): pl.pallas_call(functools.partial(kernel, n, scale), out_shape=jax.ShapeDt...  1.25 us

profile of v1, /device:TPU:0, one launch (start us, length us, event | category | flops | bytes accessed | tf_op | source)
XLA Modules:
  0.0 51.3 jit_solution(9890800299950708780)
XLA Ops:
  0.7 11.6 %copy.7.eig_ref = bf16[8192,448]{1,0:T(8,128)(2,1)} copy(bf16[8192,448]{0,1:T(8,128)(2,1)} %param.8) | data formatting | bytes 14680064 | tf_op args[2]
  12.2 37.8 %shard_map.64 = f32[4,1]{1,0:T(4,128)} custom-call(s32[1]{0:T(128)S(6)} %copy.9.len_ref, bf16[4,16,8192]{2,1,0:T(8,128)(2,1)} %qact_ref.1, bf16[4,16,448]{2,1,0:T(8,128)(2,1)} %qgrad_ref.1, bf16[8192,448]{1,0:T(8,128)(2,1)} %copy.7.eig_ref, bf16[1,6,8192]{2,1,0:T(8,128)(2,1)} %dact_ref.1, bf16[1,6,7168]{2,1,0:T(8,128)(2,1)} %dgrad_ref.1), custom_call_target="tpu_custom_call" | custom-call | tf_op jit(solution)/shard_map/pallas_call | solution.py:316
  50.1 1.3 %copy.8 = f32[4,1]{0,1:T(1,128)} copy(f32[4,1]{1,0:T(4,128)} %shard_map.64) | data formatting | bytes 32 | tf_op jit(solution)/shard_map/pallas_call | solution.py:316

commit v2 on v1

--- a/solution.py
+++ b/solution.py
@@ -19,14 +19,13 @@
 
 
 def kernel(n, scale, len_ref, qact_ref, qgrad_ref, eig_ref, dact_ref, dgrad_ref, out_ref,
-           buf, wide, actb, pre, eigv, qt, bd, own, gown, gtmp, gsend, grecv, gwide, acc, part, parts,
+           buf, wide, actb, pre, eigv, qgt, own, gown, gtmp, gsend, grecv, gwide, grads, gradt, acc, rows, part, parts,
            eig_sem, ring_send, ring_recv, cross_send, cross_recv, g_send, g_recv, p_send, p_recv):
     queries, qtokens, width = qact_ref.shape
     tokens = dact_ref.shape[1]
-    slab = eig_ref.shape[1]
+    slab = eig_ref.shape[0]
     fold = width // FOLDS
     half = fold // 2
-    full = slab // 128
     chips = n // 2
     hops = chips // 2
     groups = chips
@@ -51,7 +50,7 @@
     def eig_copy(g):
         slot = lax.rem(g, EIG_SLOTS)
         return pltpu.make_async_copy(
-            eig_ref.at[pl.ds(pl.multiple_of(g * group_rows, group_rows), group_rows)],
+            eig_ref.at[:, pl.ds(pl.multiple_of(g * group_rows, group_rows), group_rows)],
             eigv.at[slot], eig_sem.at[slot])
 
     for g in range(EIG_SLOTS - 1):
@@ -103,19 +102,29 @@
             ring_copy(way, 1, h).start()
     cross_copy(pos, core).start()
 
-    bd[...] = jnp.zeros_like(bd)
     for q in range(queries):
-        rows = slice(q * qtokens, (q + 1) * qtokens)
-        for j in range(full):
-            at = (j * queries + q) * 128
-            bd[rows, at:at + 128] = qgrad_ref[q, :, j * 128:(j + 1) * 128]
-        rest = qgrad_ref[q, :, full * 128:]
-        none = jnp.zeros_like(rest)
-        at = (full * queries + q // 2) * 128
-        bd[rows, at:at + 128] = jnp.concatenate([rest, none] if q % 2 == 0 else [none, rest], axis=1)
-    for q in range(queries):
-        rows = slice(q * qtokens, (q + 1) * qtokens)
-        qt[rows, :] = qact_ref[q]
+        qgt[q] = qgrad_ref[q].astype(f32).T.astype(bf16)
+
+    slot_of = lax.broadcasted_iota(jnp.int32, (tokens, dgrad_ref.shape[2]), 0)
+    gown[...] = jnp.where(slot_of < len_ref[0], dgrad_ref[0].astype(f32), 0.0)
+    gtmp[...] = jnp.zeros_like(gtmp)
+
+    @pl.loop(0, n)
+    def _(to):
+        start = pl.multiple_of((to * slab) // 128 * 128, 128)
+        for side in range(2):
+            for b in range(2):
+                at = pl.multiple_of(start + side * 256 + b * 128, 128)
+                gtmp[b, pl.ds(side, tokens, stride=2), :] = gown[:, pl.ds(at, 128)]
+        gsend[to] = jnp.concatenate([gtmp[0], gtmp[1]], axis=1).astype(bf16)
+
+    grecv[me] = gsend[me]
+
+    def g_copy(slot, to):
+        return pltpu.make_async_remote_copy(
+            src_ref=gsend.at[to], dst_ref=grecv.at[slot],
+            send_sem=g_send.at[to], recv_sem=g_recv.at[slot],
+            device_id={"docs": to}, device_id_type=MESH)
 
     def make_pre(g):
         slot = lax.rem(g, EIG_SLOTS)
@@ -129,18 +138,10 @@
         def _(c):
             local = pl.multiple_of(c * CHUNK, CHUNK)
             at = pl.multiple_of(g * group_rows + c * CHUNK, CHUNK)
-            left = qt[:, pl.ds(at, CHUNK)].T
-            inv = 1.0 / (eigv[slot, pl.ds(local, CHUNK), :].astype(f32) + damping)
-            tail = inv[:, full * 128:]
-            tail = jnp.concatenate([tail, tail], axis=1)
-            for pair in range(bd.shape[1] // 256):
-                cols = slice(pair * 256, pair * 256 + 256)
-                gram = jnp.dot(left, bd[:, cols], preferred_element_type=f32)
-                for side in range(2):
-                    j = (pair * 2 + side) // queries
-                    w = inv[:, j * 128:(j + 1) * 128] if j < full else tail
-                    lo = pair * 256 + side * 128
-                    pre[pl.ds(at, CHUNK), lo:lo + 128] = (gram[:, side * 128:side * 128 + 128] * w).astype(bf16)
+            inv = 1.0 / (eigv[slot, :, pl.ds(local, CHUNK)].astype(f32) + damping)
+            for q in range(queries):
+                gram = jnp.dot(qgt[q], qact_ref[q, :, pl.ds(at, CHUNK)], preferred_element_type=f32)
+                pre[q * slab:(q + 1) * slab, pl.ds(at, CHUNK)] = (gram * inv).astype(bf16)
 
     @pl.loop(0, chips - 2)
     def _(e):
@@ -167,34 +168,9 @@
             cross_copy(pos - step, core).start()
             cross_copy(pos + step, core).start()
 
-    slot_of = lax.broadcasted_iota(jnp.int32, (tokens, dgrad_ref.shape[2]), 0)
-    gown[...] = jnp.where(slot_of < len_ref[0], dgrad_ref[0].astype(f32), 0.0)
-    gtmp[...] = jnp.zeros_like(gtmp)
-
-    def g_copy(slot, to):
-        return pltpu.make_async_remote_copy(
-            src_ref=gsend.at[to], dst_ref=grecv.at[slot],
-            send_sem=g_send.at[to], recv_sem=g_recv.at[slot],
-            device_id={"docs": to}, device_id_type=MESH)
-
-    @pl.loop(0, n)
-    def _(r):
-        to = lax.rem(me + r, n)
-        start = pl.multiple_of((to * slab) // 128 * 128, 128)
-        for side in range(2):
-            for b in range(2):
-                at = pl.multiple_of(start + side * 256 + b * 128, 128)
-                gtmp[b, pl.ds(side, tokens, stride=2), :] = gown[:, pl.ds(at, 128)]
-        cut = jnp.concatenate([gtmp[0], gtmp[1]], axis=1).astype(bf16)
-        gsend[to] = cut
-
-        @pl.when(r == 0)
-        def _():
-            grecv[me] = cut
-
-        @pl.when(r > 0)
-        def _():
-            g_copy(me, to).start()
+    @pl.loop(1, n)
+    def _(r):
+        g_copy(me, lax.rem(me + r, n)).start()
 
     make_pre(chips - 2)
     ring_arrival(0, hops, 0).wait_recv()
@@ -219,12 +195,11 @@
 
     @pl.loop(0, FOLDS)
     def _(k):
-        rows = pl.ds(pl.multiple_of(k * fold, fold), fold)
         for b in range(fold // 128):
             actb[:, b * 128:(b + 1) * 128] = wide[b, pl.ds(k, tokens * n, stride=FOLDS), :].astype(bf16)
-        for pair in range(bd.shape[1] // 256):
-            cols = slice(pair * 256, pair * 256 + 256)
-            acc[:, cols] += jnp.dot(actb[...], pre[rows, cols], preferred_element_type=f32)
+        acc[...] += lax.dot_general(
+            pre[:, pl.ds(pl.multiple_of(k * fold, fold), fold)], actb[...],
+            (((1,), (1,)), ((), ())), preferred_element_type=f32)
 
     @pl.loop(1, n)
     def _(r):
@@ -237,26 +212,23 @@
             gwide[b, pl.ds(pl.multiple_of(d * 16, 16), 16), :] = got[:, b * 128:(b + 1) * 128]
 
     part[...] = jnp.zeros_like(part)
+    rows[...] = jnp.zeros_like(rows)
+    grads[...] = jnp.zeros_like(grads)
     odd = lax.rem(me, 2) == 1
-    sums = [jnp.zeros((n, 128), f32) for _ in range(queries)]
-    low = lax.broadcasted_iota(jnp.int32, (n, 128), 1) < slab - full * 128
     for t in range(tokens):
         window = jnp.concatenate(
             [gwide[b, pl.ds(t * 2 + side, n, stride=16), :] for side in range(2) for b in range(2)], axis=1)
         moved = jnp.concatenate([window[:, 64:], window[:, :64]], axis=1)
-        grad = jnp.where(odd, moved, window)
-        last = grad[:, full * 128:full * 128 + 64]
-        last = jnp.concatenate([last, last], axis=1)
-        rows = slice(t * n, (t + 1) * n)
-        for q in range(queries):
-            for j in range(full):
-                at = (j * queries + q) * 128
-                sums[q] += acc[rows, at:at + 128] * grad[:, j * 128:(j + 1) * 128]
-            at = (full * queries + q // 2) * 128
-            both = acc[rows, at:at + 128] * last
-            sums[q] += jnp.where(low if q % 2 == 0 else jnp.logical_not(low), both, 0.0)
+        grads[t * n:(t + 1) * n, :] = jnp.where(odd, moved, window)
+    gradt[...] = grads[...].T
     for q in range(queries):
-        part[pl.ds(q, n, stride=8), :] = sums[q]
+        rows[q:q + 1, :tokens * n] = jnp.sum(
+            acc[q * slab:(q + 1) * slab, :] * gradt[:slab, :tokens * n], axis=0, keepdims=True)
+    scores = rows[...].T
+    total = scores[0:n]
+    for t in range(1, tokens):
+        total += scores[t * n:(t + 1) * n]
+    part[pl.ds(0, n, stride=8), :] = total
 
     def p_copy(slot, to):
         return pltpu.make_async_remote_copy(
@@ -295,7 +267,7 @@
     total = parts[0:8, :]
     for d in range(1, n):
         total += parts[d * 8:d * 8 + 8, :]
-    out_ref[...] = jnp.sum(total, axis=1, keepdims=True)[:queries] * scale
+    out_ref[...] = total[0:1, :queries] * scale
 
     @pl.loop(1, n)
     def _(r):
@@ -310,29 +282,32 @@
     chips = n // 2
     fold = width // FOLDS
     columns = queries * slab
+    padded = -(-n * tokens // 128) * 128
     scale = 1.0 / (5.0 * math.sqrt(qtokens * width * slab * n * tokens))
     vmem = pl.BlockSpec(memory_space=pltpu.VMEM)
     dma = pltpu.SemaphoreType.DMA
     return pl.pallas_call(
         functools.partial(kernel, n, scale),
-        out_shape=jax.ShapeDtypeStruct((queries, 1), f32),
+        out_shape=jax.ShapeDtypeStruct((1, queries), f32),
         in_specs=[pl.BlockSpec(memory_space=pltpu.SMEM), vmem, vmem, pl.BlockSpec(memory_space=pl.ANY), vmem, vmem],
         out_specs=vmem,
         scratch_shapes=[
             pltpu.VMEM((n, tokens * FOLDS, fold), bf16),
             pltpu.VMEM((fold // 128, n * tokens * FOLDS, 128), f32),
             pltpu.VMEM((n * tokens, fold), bf16),
-            pltpu.VMEM((width, columns), bf16),
-            pltpu.VMEM((EIG_SLOTS, width // chips, slab), bf16),
-            pltpu.VMEM((queries * qtokens, width), bf16),
-            pltpu.VMEM((queries * qtokens, columns), bf16),
+            pltpu.VMEM((columns, width), bf16),
+            pltpu.VMEM((EIG_SLOTS, slab, width // chips), bf16),
+            pltpu.VMEM((queries, slab, qtokens), bf16),
             pltpu.VMEM((fold // 128, tokens * FOLDS, 128), f32),
             pltpu.VMEM((tokens, doc_grad.shape[2]), f32),
             pltpu.VMEM((2, 16, 128), f32),
             pltpu.VMEM((n, 16, 256), bf16),
             pltpu.VMEM((n, 16, 256), bf16),
             pltpu.VMEM((2, n * 16, 128), f32),
-            pltpu.VMEM((n * tokens, columns), f32),
+            pltpu.VMEM((padded, 512), f32),
+            pltpu.VMEM((512, padded), f32),
+            pltpu.VMEM((columns, n * tokens), f32),
+            pltpu.VMEM((128, padded), f32),
             pltpu.VMEM((n * 8, 128), f32),
             pltpu.VMEM((n * 8, 128), f32),
             dma((EIG_SLOTS,)),
@@ -347,7 +322,7 @@
         ],
         compiler_params=pltpu.CompilerParams(
             collective_id=0, has_side_effects=True, vmem_limit_bytes=62 * 1024 * 1024),
-    )(doc_len, query_act, query_grad, eigenvalues, doc_act, doc_grad)
+    )(doc_len, query_act, query_grad, eigenvalues.T, doc_act, doc_grad).T
 
 
 def solution(mesh):

time: 51.8 us -> 42.2 us (0.81)
  local copies, waits for them, and re-layouts: 12.8 us -> 1.19 us
  Pallas kernels: 37.8 us -> 40.2 us
    unnamed x1, local copies, waits for them, and re-layouts: 11.6 us -> 1.19 us
    pallas_call x1, Pallas kernels: 37.8 us -> 40.2 us  [body(): pl.pallas_call(functools.partial(kernel, n, scale), out_shape=jax.ShapeDt...]
    pallas_call x1 -> x0, local copies, waits for them, and re-layouts: 1.25 us -> none  [body(): pl.pallas_call(functools.partial(kernel, n, scale), out_shape=jax.ShapeDt...]
where the time goes in v2:
time: 42.2 us; the launch traced here: 42 us
  Pallas kernels  40.2 us (95%)
  local copies, waits for them, and re-layouts  1.19 us (3%)
  between operations  0.66 us (2%)
    pallas_call x1, Pallas kernels, body(): pl.pallas_call(functools.partial(kernel, n, scale), out_shape=jax.ShapeDt...  40.2 us
    unnamed x1, local copies, waits for them, and re-layouts  1.19 us

profile of v2, /device:TPU:0, one launch (start us, length us, event | category | flops | bytes accessed | tf_op | source)
XLA Modules:
  0.0 42.0 jit_solution(15878400517198390753)
XLA Ops:
  0.7 40.2 %shard_map.64 = f32[1,4]{1,0:T(1,128)} custom-call(s32[1]{0:T(128)S(6)} %copy.8.len_ref, bf16[4,16,8192]{2,1,0:T(8,128)(2,1)} %qact_ref.1, bf16[4,16,448]{2,1,0:T(8,128)(2,1)} %qgrad_ref.1, bf16[448,8192]{1,0:T(8,128)(2,1)} %bitcast.2, bf16[1,6,8192]{2,1,0:T(8,128)(2,1)} %dact_ref.1, bf16[1,6,7168]{2,1,0:T(8,128)(2,1)} %dgrad_ref.1), custom_call_target="tpu_custom_call" | custom-call | tf_op jit(solution)/shard_map/pallas_call | solution.py:289
  40.8 1.2 %copy.9 = f32[4,1]{0,1:T(1,128)} copy(f32[4,1]{0,1:T(1,128)} %bitcast.3) | data formatting | bytes 32
